TPU v7x, 256 devices: a whole 4x4x8 slice. The times are simulated.
256 devices in a mesh: expert: 64 (over y, z, core), half: 4 (over x).
Axes of the slice: x: 4, y: 4, z: 8, core: 2. Of those that a mesh axis runs over, the one named last changes fastest.
Arguments:
- tokens: bfloat16 [16384, 2048], P('expert', 'half'), may hold values from -6 to 6
- out_grad: bfloat16 [16384, 2048], P('expert', 'half'), may hold values from -6 to 6
- w_gate: bfloat16 [128, 768, 2048], P('expert', 'half'), may hold values from -0.125 to 0.125
- w_up: bfloat16 [128, 768, 2048], P('expert', 'half'), may hold values from -0.125 to 0.125
- w_down: bfloat16 [128, 768, 2048], P('expert', 'half'), may hold values from -0.21875 to 0.21875
- chosen_rows: int32 [128, 64, 8], P(None, 'expert'), may hold values from 0 to 255, as said below
- counts: int32 [128, 64], P(None, 'expert'), may hold values from 1 to 8, 256 in all within a row
- gate_values: bfloat16 [128, 64, 8], P(None, 'expert'), may hold values from 0.099609375 to 1
Outputs:
- grad_tokens: bfloat16 [16384, 2048], P('expert', 'half')
- grad_w_gate: bfloat16 [128, 768, 2048], P('expert', 'half')
- grad_w_up: bfloat16 [128, 768, 2048], P('expert', 'half')
- grad_w_down: bfloat16 [128, 768, 2048], P('expert', 'half')
- gate_grad: bfloat16 [128, 64, 8], P(None, 'expert')
Inputs may be any that keep to these rules, and one draw needn't show every extreme that they name: `chosen_rows`: for each expert and token group the first counts entries are distinct positions in the group of 256 tokens; entries past counts are positions too and are unused. For each expert the counts over all token groups sum to 256.
All inputs are finite; a program needn't handle non-finite values.
Results may differ from a plain program's by a relative error of at most 0.017.
Values may be sent and summed in bfloat16 or wider, within the bound.
A program may use at most 128 MiB of HBM per device.

v0:
```python
import jax
import jax.numpy as jnp
from jax import lax
from jax.sharding import PartitionSpec as P


def body(tokens, out_grad, w_gate, w_up, w_down, chosen_rows, counts, gate_values):
    tok_dev = tokens.shape[0]
    quarter = tokens.shape[1]
    experts = chosen_rows.shape[0]
    slot_most = chosen_rows.shape[2]
    slots_flat = chosen_rows.reshape(-1)
    live_slots = lax.broadcasted_iota(jnp.int32, (experts, slot_most), 1) < counts
    gate_send = jnp.where(
        live_slots, gate_values.reshape(experts, slot_most), jnp.zeros((), gate_values.dtype)
    )
    token_send = jnp.take(tokens, slots_flat, axis=0).reshape(experts, slot_most, quarter)
    grad_send = jnp.take(out_grad, slots_flat, axis=0).reshape(experts, slot_most, quarter)
    token_recv, grad_recv, gate_recv = (
        lax.all_to_all(token_send, "expert", split_axis=0, concat_axis=1, tiled=True),
        lax.all_to_all(grad_send, "expert", split_axis=0, concat_axis=1, tiled=True),
        lax.all_to_all(gate_send, "expert", split_axis=0, concat_axis=1, tiled=True),
    )
    x_rows, dy_rows = (
        lax.all_gather(token_recv, "half", axis=2, tiled=True),
        lax.all_gather(grad_recv, "half", axis=2, tiled=True),
    )
    pre_gate = jnp.einsum("erd,efd->erf", x_rows, w_gate, preferred_element_type=jnp.float32)
    pre_up = jnp.einsum("erd,efd->erf", x_rows, w_up, preferred_element_type=jnp.float32)
    back_proj = jnp.einsum("erd,efd->erf", dy_rows, w_down, preferred_element_type=jnp.float32)
    sigmoid_gate = jax.nn.sigmoid(pre_gate)
    activated = pre_gate * sigmoid_gate
    hidden = (activated * pre_up).astype(jnp.bfloat16)
    scaled = gate_recv[:, :, None] * dy_rows
    slot_sums = jnp.sum(hidden.astype(jnp.float32) * back_proj, axis=2)
    gate_grad_rows = lax.psum(slot_sums, "half").astype(jnp.bfloat16)
    d_hidden = gate_recv.astype(jnp.float32)[:, :, None] * back_proj
    d_gate = (d_hidden * pre_up * sigmoid_gate * (1.0 + pre_gate * (1.0 - sigmoid_gate))).astype(
        jnp.bfloat16
    )
    d_up = (d_hidden * activated).astype(jnp.bfloat16)
    grad_w_down = jnp.einsum(
        "erf,erd->efd", hidden, scaled, preferred_element_type=jnp.float32
    ).astype(jnp.bfloat16)
    grad_w_gate = jnp.einsum(
        "erf,erd->efd", d_gate, x_rows, preferred_element_type=jnp.float32
    ).astype(jnp.bfloat16)
    grad_w_up = jnp.einsum("erf,erd->efd", d_up, x_rows, preferred_element_type=jnp.float32).astype(
        jnp.bfloat16
    )
    partial_value = jnp.einsum(
        "erf,efd->erd", d_gate, w_gate, preferred_element_type=jnp.float32
    ) + jnp.einsum("erf,efd->erd", d_up, w_up, preferred_element_type=jnp.float32)
    row_grad = lax.psum_scatter(
        partial_value.astype(jnp.bfloat16), "half", scatter_dimension=2, tiled=True
    )
    rows_home, gate_home = (
        lax.all_to_all(row_grad, "expert", split_axis=1, concat_axis=0, tiled=True),
        lax.all_to_all(gate_grad_rows, "expert", split_axis=1, concat_axis=0, tiled=True),
    )
    one_hot = (slots_flat[None, :] == lax.broadcasted_iota(jnp.int32, (tok_dev, 1), 0)).astype(
        jnp.bfloat16
    )
    grad_tokens = jnp.dot(
        one_hot, rows_home.reshape(experts * slot_most, quarter), preferred_element_type=jnp.float32
    ).astype(jnp.bfloat16)
    gate_grad = (gate_home * live_slots.astype(jnp.bfloat16)).reshape(experts, 1, slot_most)
    return (grad_tokens, grad_w_gate, grad_w_up, grad_w_down, gate_grad)


def solution(mesh):
    return jax.shard_map(
        body,
        mesh=mesh,
        in_specs=(
            P("expert", "half"),
            P("expert", "half"),
            P("expert", "half", None),
            P("expert", "half", None),
            P("expert", "half", None),
            P(None, "expert", None),
            P(None, "expert"),
            P(None, "expert", None),
        ),
        out_specs=(
            P("expert", "half"),
            P("expert", "half", None),
            P("expert", "half", None),
            P("expert", "half", None),
            P(None, "expert", None),
        ),
        check_vma=False,
    )
```

profile of v0, /device:TPU:1, one launch (start us, length us, event | category | flops | bytes accessed | tf_op | source)
XLA Modules:
  0.0 275.9 jit_solution(8268832146259380280)
XLA Ops:
  7.2 0.0 copy-start
  7.2 0.0 all-gather.5.cloned.1.call-start
  7.2 0.9 copy.30
  8.1 0.1 eq.15
  8.2 0.0 copy-start.1
  8.3 5.0 %gather_fusion.1 = bf16[1024,512]{1,0:T(8,128)(2,1)S(1)} fusion(bf16[256,512]{1,0:T(8,128)(2,1)} %param.10, s32[1024]{0:T(1024)S(1)} %fusion.9), kind=kCustom, calls=%fused_computation.1.clone | custom fusion | bytes 2101248 | tf_op jit(solution)/shard_map/jit(_take)/gather | solution.py:17
  13.3 0.0 copy-done.1
  13.3 5.1 %gather_fusion = bf16[1024,512]{1,0:T(8,128)(2,1)} fusion(bf16[256,512]{1,0:T(8,128)(2,1)S(1)} %copy-done.1, s32[1024]{0:T(1024)S(1)} %fusion.9), kind=kCustom, calls=%fused_computation.clone | custom fusion | bytes 2101248 | tf_op jit(solution)/shard_map/jit(_take)/gather | solution.py:18
  18.4 2.5 select_bitcast_fusion.1
  20.8 41.6 %all_to_all.86 = bf16[128,8,512]{2,1,0:T(8,128)(2,1)S(1)} all-to-all(bf16[128,8,512]{2,1,0:T(8,128)(2,1)S(1)} %get-tuple-element.26), channel_id=1, replica_groups=mesh['expert'=64,'half'=4] {'expert'}, dimensions={0} | all-to-all | bytes 2097152 | tf_op jit(solution)/shard_map/all_to_all | solution.py:20
  62.5 0.0 copy-start.9
  62.5 1.1 copy.44
  63.5 0.0 all-gather.5.cloned.1.call-update
  63.6 0.0 all-gather.3.cloned.1.call-start
  63.6 0.0 copy-done.5
  63.6 34.5 %all_to_all.87 = bf16[128,8,512]{2,1,0:T(8,128)(2,1)S(1)} all-to-all(bf16[128,8,512]{2,1,0:T(8,128)(2,1)S(1)} %copy-done.5), channel_id=1, replica_groups=mesh['expert'=64,'half'=4] {'expert'}, dimensions={0} | all-to-all | bytes 2097152 | tf_op jit(solution)/shard_map/all_to_all | solution.py:21
  98.2 1.1 copy.45
  99.2 0.0 all-gather.3.cloned.1.call-update
  99.2 0.0 reduce-scatter.2.cloned.1.call-start
  99.3 0.5 broadcast.56
  99.8 0.0 copy-done.9
  99.8 0.7 reduce.3
  100.5 0.1 lt.28
  100.6 0.0 copy-done.8
  100.6 0.1 copy.31
  100.7 0.1 compare_select_fusion
  100.9 15.3 %all_to_all.88 = bf16[64,2,8]{2,1,0:T(2,128)(2,1)S(1)} all-to-all(bf16[64,2,8]{2,1,0:T(2,128)(2,1)S(1)} %compare_select_fusion), channel_id=1, replica_groups=mesh['expert'=64,'half'=4] {'expert'}, dimensions={0} | all-to-all | bytes 4096 | tf_op jit(solution)/shard_map/all_to_all | solution.py:22
  116.2 0.1 all_to_all.65
  116.3 0.0 all-gather.5.cloned.1.call-done
  116.3 0.0 copy-done
  116.3 0.0 copy-start.2
  116.3 4.8 %fusion.11 = f32[2,512,192]{1,2,0:T(8,128)} fusion(bf16[2,512,2048]{2,1,0:T(8,128)(2,1)} %all-gather.5.cloned.1.call-done, bf16[2,192,2048]{2,1,0:T(8,128)(2,1)S(1)} %copy-done), kind=kOutput, calls=%fused_computation.30 | convolution fusion | flops 805306368 | bytes 6553600 | tf_op jit(solution)/shard_map/erd,efd->erf/dot_general | solution.py:28
  121.1 0.0 copy-done.4
  121.1 0.0 copy-done.2
  121.1 2.5 fusion.10
  123.6 41.3 %all-gather.3.cloned.1.call-done = bf16[2,512,2048]{2,1,0:T(8,128)(2,1)} async-done(((bf16[2,512,512]{2,1,0:T(8,128)(2,1)}), bf16[2,512,2048]{2,1,0:T(8,128)(2,1)}) %all-gather.3.cloned.1.call-update) | async-done | bytes 4194320 | tf_op jit(solution)/shard_map/all_gather | solution.py:26
  164.9 5.6 %multiply_reduce_fusion = (f32[2,512]{1,0:T(2,128)S(1)}, bf16[2,512,192]{1,2,0:T(8,128)(2,1)}, bf16[2,512,192]{1,2,0:T(8,128)(2,1)S(1)}, bf16[2,512,192]{1,2,0:T(8,128)(2,1)S(1)}) fusion(f32[2,512,192]{1,2,0:T(8,128)} %fusion.10, f32[2,512,192]{1,2,0:T(8,128)} %fusion.11, f32[2,512]{1,0:T(2,128)S(1)} %convert_element_type.39, ...), kind=kOutput, calls=%fused_computation.16 | convolution fusion | flops 809040896 | bytes 8527872 | tf_op jit(solution)/shard_map/erd,efd->erf/dot_general | solution.py:30
  170.5 1.3 fusion.12
  171.8 0.0 copy-done.6
  171.8 3.4 %add_convert_fusion = bf16[2,512,2048]{2,1,0:T(8,128)(2,1)} fusion(f32[2,512,2048]{2,1,0:T(8,128)S(1)} %fusion.12, bf16[2,512,192]{1,2,0:T(8,128)(2,1)S(1)} %get-tuple-element.24, bf16[2,192,2048]{2,1,0:T(8,128)(2,1)S(1)} %copy-done.4), kind=kOutput, calls=%fused_computation.2 | convolution fusion | flops 809500672 | bytes 14548992 | tf_op jit(solution)/shard_map/erf,efd->erd/dot_general | solution.py:53
  175.2 0.0 reduce-scatter.2.cloned.1.call-update
  175.2 6.6 %psum.7 = bf16[2,512]{1,0:T(2,128)(2,1)S(1)} all-reduce(f32[2,512]{1,0:T(2,128)S(1)} %get-tuple-element.21), channel_id=1, replica_groups=mesh['expert'=64,'half'=4] {'half'}, use_global_device_ids=true, to_apply=%region_2.4 | all-reduce | flops 1024 | bytes 6144 | tf_op jit(solution)/shard_map/psum | solution.py:36
  181.9 0.1 all_to_all.77
  182.0 0.7 copy.38
  182.6 13.0 %all-to-all-start.4 = ((bf16[2,64,8]{2,0,1:T(2,128)(2,1)}), bf16[2,64,8]{2,0,1:T(2,128)(2,1)S(1)}, u32[]{:S(2)}, u32[]{:S(2)}) async-start(bf16[2,64,8]{2,0,1:T(2,128)(2,1)} %copy.38), calls=%async_computation.5 | async-start | bytes 65536 | tf_op jit(solution)/shard_map/all_to_all | solution.py:59
  195.6 29.6 %reduce-scatter.2.cloned.1.call-done = bf16[2,512,512]{2,1,0:T(8,128)(2,1)} async-done(((bf16[2,512,2048]{2,1,0:T(8,128)(2,1)}), bf16[2,512,512]{2,1,0:T(8,128)(2,1)}) %reduce-scatter.2.cloned.1.call-update) | async-done | bytes 1048592 | tf_op jit(solution)/shard_map/reduce_scatter | solution.py:54
  225.2 3.4 %copy.35 = bf16[2,512,512]{2,0,1:T(2,128)(2,1)} copy(bf16[2,512,512]{2,1,0:T(8,128)(2,1)} %reduce-scatter.2.cloned.1.call-done) | data formatting | bytes 2097152 | tf_op jit(solution)/shard_map/reduce_scatter | solution.py:54
  228.6 0.0 all-to-all-done.4
  228.6 10.8 %all-to-all-start.3 = ((bf16[2,512,512]{2,0,1:T(2,128)(2,1)}), bf16[2,512,512]{2,0,1:T(2,128)(2,1)S(1)}, u32[]{:S(2)}, u32[]{:S(2)}) async-start(bf16[2,512,512]{2,0,1:T(2,128)(2,1)} %copy.35), calls=%async_computation.4 | async-start | bytes 2097152 | tf_op jit(solution)/shard_map/all_to_all | solution.py:58
  239.4 0.0 copy-start.3
  239.4 4.5 %convolution_convert_fusion.1 = bf16[2,192,2048]{2,1,0:T(8,128)(2,1)} fusion(bf16[2,512,192]{1,2,0:T(8,128)(2,1)S(1)} %get-tuple-element.23, bf16[2,512,2048]{2,1,0:T(8,128)(2,1)} %all-gather.5.cloned.1.call-done), kind=kOutput, calls=%fused_computation.7 | convolution fusion | flops 806092800 | bytes 6160384 | tf_op jit(solution)/shard_map/erf,erd->efd/dot_general | solution.py:45
  243.8 0.0 copy-done.7
  243.9 0.0 copy-done.3
  243.9 2.1 convolution_convert_fusion
  246.0 0.6 copy-done.11
  246.6 0.1 copy-done.12
  246.7 2.3 fusion.2
  249.0 0.0 copy-done.10
  249.0 0.1 fusion.8
  249.1 0.7 copy.39
  249.7 18.2 %all-to-all-done.3 = bf16[2,512,512]{2,0,1:T(2,128)(2,1)S(1)} async-done(((bf16[2,512,512]{2,0,1:T(2,128)(2,1)}), bf16[2,512,512]{2,0,1:T(2,128)(2,1)S(1)}, u32[]{:S(2)}, u32[]{:S(2)}) %all-to-all-start.3) | async-done | bytes 1048608 | tf_op jit(solution)/shard_map/all_to_all | solution.py:58
  267.9 0.2 copy.43
  268.1 0.1 copy.37
  268.2 1.2 convolution_convert_fusion.2
  (12 shorter events, 0.0 us)
Async XLA Ops:
  7.2 109.2 %copy-start = (bf16[2,192,2048]{2,1,0:T(8,128)(2,1)S(1)}, bf16[2,192,2048]{2,1,0:T(8,128)(2,1)}, u32[]{:S(2)}) copy-start(bf16[2,192,2048]{2,1,0:T(8,128)(2,1)} %param.12) | copy-start | bytes 4718596
  7.2 109.1 %all-gather.5.cloned.1.call-start = ((), (), s32[]{:S(2)}) async-start(), calls=%async_computation.7 | async-start | bytes 5242880 | tf_op jit(solution)/shard_map/all_gather | solution.py:25
  8.2 5.0 %copy-start.1 = (bf16[256,512]{1,0:T(8,128)(2,1)S(1)}, bf16[256,512]{1,0:T(8,128)(2,1)}, u32[]{:S(2)}) copy-start(bf16[256,512]{1,0:T(8,128)(2,1)} %param.11) | copy-start | bytes 786436
  20.8 42.8 %copy-start.5 = (bf16[128,8,512]{2,1,0:T(8,128)(2,1)S(1)}, bf16[128,8,512]{2,1,0:T(8,128)(2,1)}, u32[]{:S(2)}) copy-start(bf16[128,8,512]{2,1,0:T(8,128)(2,1)} %get-tuple-element.25) | copy-start | bytes 3145732
  62.5 37.3 %copy-start.9 = (s32[128,1]{0,1:T(1,128)S(1)}, s32[128,1]{0,1:T(1,128)}, u32[]{:S(2)}) copy-start(s32[128,1]{0,1:T(1,128)} %param.16) | copy-start | bytes 1540
  62.5 38.1 %copy-start.8 = (bf16[128,1,8]{0,2,1:T(8,128)(2,1)S(1)}, bf16[128,1,8]{0,2,1:T(8,128)(2,1)}, u32[]{:S(2)}) copy-start(bf16[128,1,8]{0,2,1:T(8,128)(2,1)} %param.17) | copy-start | bytes 6148
  63.6 101.3 %all-gather.3.cloned.1.call-start = ((), (), s32[]{:S(2)}) async-start(), calls=%async_computation.6 | async-start | bytes 5242880 | tf_op jit(solution)/shard_map/all_gather | solution.py:26
  99.2 21.9 %copy-start.4 = (bf16[2,192,2048]{2,1,0:T(8,128)(2,1)S(1)}, bf16[2,192,2048]{2,1,0:T(8,128)(2,1)}, u32[]{:S(2)}) copy-start(bf16[2,192,2048]{2,1,0:T(8,128)(2,1)} %param.13) | copy-start | bytes 4718596
  99.2 126.0 %reduce-scatter.2.cloned.1.call-start = ((), (), s32[]{:S(2)}) async-start(), calls=%async_computation.8 | async-start | bytes 5242880 | tf_op jit(solution)/shard_map/reduce_scatter | solution.py:54
  116.3 4.8 %copy-start.2 = (bf16[2,512,2048]{2,1,0:T(8,128)(2,1)S(1)}, bf16[2,512,2048]{2,1,0:T(8,128)(2,1)}, u32[]{:S(2)}) copy-start(bf16[2,512,2048]{2,1,0:T(8,128)(2,1)} %all-gather.5.cloned.1.call-done) | copy-start | bytes 12582916
  170.5 1.3 copy-start.6
  182.6 45.9 %all-to-all-start.4 = ((bf16[2,64,8]{2,0,1:T(2,128)(2,1)}), bf16[2,64,8]{2,0,1:T(2,128)(2,1)S(1)}, u32[]{:S(2)}, u32[]{:S(2)}) async-start(bf16[2,64,8]{2,0,1:T(2,128)(2,1)} %copy.38), calls=%async_computation.5 | async-start | bytes 65536 | tf_op jit(solution)/shard_map/all_to_all | solution.py:59
  228.6 15.3 %copy-start.7 = (bf16[2,512,192]{1,2,0:T(8,128)(2,1)S(1)}, bf16[2,512,192]{1,2,0:T(8,128)(2,1)}, u32[]{:S(2)}) copy-start(bf16[2,512,192]{1,2,0:T(8,128)(2,1)} %copy-done.6) | copy-start | bytes 1179652
  228.6 39.3 %all-to-all-start.3 = ((bf16[2,512,512]{2,0,1:T(2,128)(2,1)}), bf16[2,512,512]{2,0,1:T(2,128)(2,1)S(1)}, u32[]{:S(2)}, u32[]{:S(2)}) async-start(bf16[2,512,512]{2,0,1:T(2,128)(2,1)} %copy.35), calls=%async_computation.4 | async-start | bytes 2097152 | tf_op jit(solution)/shard_map/all_to_all | solution.py:58
  239.4 4.5 %copy-start.3 = (bf16[2,512,2048]{2,1,0:T(8,128)(2,1)S(1)}, bf16[2,512,2048]{2,1,0:T(8,128)(2,1)}, u32[]{:S(2)}) copy-start(bf16[2,512,2048]{2,1,0:T(8,128)(2,1)} %all-gather.5.cloned.1.call-done) | copy-start | bytes 12582916
  243.9 2.8 copy-start.11
  243.9 2.8 %copy-start.12 = (bf16[2,512,192]{1,2,0:T(8,128)(2,1)S(1)}, bf16[2,512,192]{1,2,0:T(8,128)(2,1)}, u32[]{:S(2)}) copy-start(bf16[2,512,192]{1,2,0:T(8,128)(2,1)} %get-tuple-element.22) | copy-start | bytes 1179652
  246.0 3.0 %copy-start.10 = (s32[128,1]{0,1:T(1,128)S(1)}, s32[128,1]{0,1:T(1,128)}, u32[]{:S(2)}) copy-start(s32[128,1]{0,1:T(1,128)} %param.16) | copy-start | bytes 1540
Sparse Core Ops, SparseCore 0:
  63.7 47.5 all-gather.4
  113.7 51.1 all-gather.2
  175.4 49.7 reduce-scatter.1
where the time goes:
time: 276 us
  blocking collectives  98.1 us (36%)
  waiting for transfers between devices  89.1 us (32%)
  matrix products  27.6 us (10%)
  starting transfers between devices  23.9 us (9%)
  local copies, waits for them, and re-layouts  19.9 us (7%)
  between operations  13.9 us (5%)
  other arithmetic  3.37 us (1%)
    all_to_all x1, blocking collectives, body(): lax.all_to_all(token_send, 'expert', split_axis=0, concat_axis=1, tiled=T...  41.6 us
    all_gather x1, waiting for transfers between devices, body(): lax.all_gather(grad_recv, 'half', axis=2, tiled=True)  41.3 us
    all_to_all x1, blocking collectives, body(): lax.all_to_all(grad_send, 'expert', split_axis=0, concat_axis=1, tiled=True)  34.5 us
    reduce_scatter x1, waiting for transfers between devices, body(): lax.psum_scatter(partial_value.astype(jnp.bfloat16), 'half', scatter_dime...  29.6 us
    all_to_all x1, waiting for transfers between devices, body(): lax.all_to_all(row_grad, 'expert', split_axis=1, concat_axis=0, tiled=True)  18.2 us
    all_to_all x1, blocking collectives, body(): lax.all_to_all(gate_send, 'expert', split_axis=0, concat_axis=1, tiled=True)  15.3 us
    all_to_all x1, starting transfers between devices, body(): lax.all_to_all(gate_grad_rows, 'expert', split_axis=1, concat_axis=0, til...  13 us
    all_to_all x1, starting transfers between devices, body(): lax.all_to_all(row_grad, 'expert', split_axis=1, concat_axis=0, tiled=True)  10.8 us
  transfers between devices with their start and end apart: 5, of which 3 were waited for; matrix products, arithmetic and copies ran while one was open for 9% of the time, Pallas kernels for 0%

commit v1 on v0

v1 whole, which is shorter than its diff:
```python
import functools

import jax
import jax.numpy as jnp
from jax import lax
from jax.experimental import pallas as pl
from jax.experimental.pallas import tpu as pltpu
from jax.sharding import PartitionSpec as P

MESH = pl.DeviceIdType.MESH
F32, BF16 = jnp.float32, jnp.bfloat16


def iota(shape, dim):
    return lax.broadcasted_iota(jnp.int32, shape, dim)


def dot(a, b, dims=((1,), (0,)), precision=None):
    return lax.dot_general(a, b, (dims, ((), ())), preferred_element_type=F32, precision=precision)


def kernel(
    n_src, n_half,
    tok, out_grad, chosen, counts, gates, wg_hbm, wu_hbm, wd_hbm,
    gt_out, gwg_out, gwu_out, gwd_out, gg_out,
    w_buf, w_sem,
    cnt_send, cnt_recv, fwd_send, fwd_recv,
    home_g, pack, spread,
    rows_all, part_send, part_recv, part_own,
    gg_part, gg_recv, ggh_send, ggh_recv,
    ret_send, ret_recv, grads, grad_sem,
    cnt_ss, cnt_rs, fwd_ss, fwd_rs, ag_ss, ag_rs, rs_ss, rs_rs,
    ggx_ss, ggx_rs, ret_ss, ret_rs, ggh_ss, ggh_rs,
):
    me = lax.axis_index("expert")
    half = lax.axis_index("half")
    tokens = tok.shape[0]
    quarter = tok.shape[1]
    fold = quarter // 2
    slots = n_src * 16
    cap = rows_all.shape[3]
    hid = wg_hbm.shape[1]

    barrier = pltpu.get_barrier_semaphore()

    @pl.loop(1, n_src)
    def _(i):
        pl.semaphore_signal(barrier, inc=1, device_id={"expert": lax.rem(me + i, n_src)}, device_id_type=MESH)

    for i in range(1, n_half):
        pl.semaphore_signal(barrier, inc=1, device_id={"half": lax.rem(half + i, n_half)}, device_id_type=MESH)

    loads = [
        pltpu.make_async_copy(ref, w_buf.at[k], w_sem.at[k]) for k, ref in enumerate((wg_hbm, wu_hbm, wd_hbm))
    ]
    for load in loads:
        load.start()

    experts, most = chosen.shape
    live = iota((experts, most), 1) < counts[...]
    chosen_live = jnp.where(live, chosen[...], -1).astype(F32).astype(BF16)
    gates_live = jnp.where(live, gates[...].astype(F32), 0.0).astype(BF16)

    count_wide = jnp.broadcast_to(counts[...].astype(F32), (experts, 128)).astype(BF16)
    lane = iota((n_src, 128), 1)
    rows_to = jnp.zeros((n_src, 128), F32)
    for e in range(2):
        pick = (iota((n_src, experts), 1) == 2 * iota((n_src, experts), 0) + e).astype(BF16)
        rows_to = rows_to + jnp.where(lane == e, dot(pick, count_wide), 0.0)
    cnt_send[...] = rows_to.reshape(n_src, 1, 128)

    def send_all(src, dst, ss, rs):
        @pl.loop(1, n_src)
        def _(i):
            to = lax.rem(me + i, n_src)
            pltpu.make_async_remote_copy(
                src_ref=src.at[to], dst_ref=dst.at[me], send_sem=ss, recv_sem=rs,
                device_id={"expert": to}, device_id_type=MESH,
            ).start()

    def wait_all(buf, sem):
        part = buf.at[pl.ds(0, n_src - 1)]
        pltpu.make_async_copy(part, part, sem).wait()

    low = (iota((slots, fold), 0) // 8) % 2 == 0
    col_pick = [
        (iota((slots, experts), 1) == 2 * (iota((slots, experts), 0) // 16) + e).astype(BF16) for e in range(2)
    ]
    slot_j = iota((slots, most), 1) == iota((slots, most), 0) % 8
    ones = jnp.ones((most, tokens), BF16)

    def spread_column(e, table):
        picked = jnp.where(slot_j, dot(col_pick[e], table), 0.0).astype(BF16)
        return dot(picked, ones)

    def folded(wide):
        return jnp.where(low, wide[:, :fold], wide[:, fold:])

    hot = [spread_column(e, chosen_live) == iota((slots, tokens), 1).astype(F32) for e in range(2)]

    def fill(k, picker, src):
        block = folded(dot(picker, src[...])).astype(BF16).reshape(n_src, 16, fold)
        fwd_send[k] = block

    fill(0, hot[0].astype(BF16), tok)
    pl.semaphore_wait(barrier, n_src - 1 + n_half - 1)
    send_all(cnt_send, cnt_recv, cnt_ss, cnt_rs)
    send_all(fwd_send.at[0], fwd_recv.at[0], fwd_ss.at[0], fwd_rs.at[0])
    fill(1, hot[1].astype(BF16), tok)
    send_all(fwd_send.at[1], fwd_recv.at[1], fwd_ss.at[1], fwd_rs.at[1])
    for e in range(2):
        fill(2 + e, jnp.where(hot[e], spread_column(e, gates_live), 0.0).astype(BF16), out_grad)
        send_all(fwd_send.at[2 + e], fwd_recv.at[2 + e], fwd_ss.at[2 + e], fwd_rs.at[2 + e])
    cnt_recv[me] = cnt_send[me]
    for k in range(4):
        fwd_recv[k, me] = fwd_send[k, me]

    wide_chosen = dot(chosen_live, (iota((most, slots), 0) == iota((most, slots), 1) % 8).astype(BF16))
    in_fold = (iota((tokens, slots), 1) // 8) % 2
    for e in range(2):
        mine = iota((experts, slots), 0) == 2 * (iota((experts, slots), 1) // 16) + e
        row = jnp.sum(jnp.where(mine, wide_chosen, 0.0), axis=0, keepdims=True)
        hit = row == iota((tokens, slots), 0).astype(F32)
        for f in range(2):
            home_g[e, f] = jnp.where(hit & (in_fold == f), 1.0, 0.0).astype(BF16)

    wait_all(cnt_recv, cnt_rs)
    count_all = cnt_recv[...].reshape(n_src, 128).astype(BF16)
    for e in range(2):
        by_col = dot(count_all, (iota((128, slots), 0) == e).astype(BF16))
        src_of = iota((n_src, slots), 1) // 16
        before = jnp.sum(jnp.where(iota((n_src, slots), 0) < src_of, by_col, 0.0), axis=0, keepdims=True)
        size = jnp.sum(jnp.where(iota((n_src, slots), 0) == src_of, by_col, 0.0), axis=0, keepdims=True)
        j = (iota((1, slots), 1) % 8).astype(F32)
        place = jnp.where(j < size, before + j, -1.0)
        hit = place == iota((cap, slots), 0).astype(F32)
        in_fold_r = (iota((cap, slots), 1) // 8) % 2
        for f in range(2):
            pack[e, f] = jnp.where(hit & (in_fold_r == f), 1.0, 0.0).astype(BF16)
        own_wide = dot(count_all, (iota((128, cap), 0) == e).astype(BF16)).astype(BF16)
        src_row = iota((slots, n_src), 0) // 16
        before_c = dot((iota((slots, n_src), 1) < src_row).astype(BF16), own_wide)
        size_c = dot((iota((slots, n_src), 1) == src_row).astype(BF16), own_wide)
        j_c = (iota((slots, cap), 0) % 8).astype(F32)
        place_c = jnp.where(j_c < size_c, before_c + j_c, -1.0)
        spread[e] = jnp.where(place_c == iota((slots, cap), 1).astype(F32), 1.0, 0.0).astype(BF16)

    def gather_copies(a, e):
        k = 2 * a + e
        return [
            pltpu.make_async_remote_copy(
                src_ref=rows_all.at[a, e, half], dst_ref=rows_all.at[a, e, half],
                send_sem=ag_ss.at[k], recv_sem=ag_rs.at[k],
                device_id={"half": lax.rem(half + i, n_half)}, device_id_type=MESH,
            )
            for i in (2, 1, 3)
        ]

    def take_in(a, e):
        k = 2 * a + e
        wait_all(fwd_recv.at[k], fwd_rs.at[k])
        got = fwd_recv[k].reshape(slots, fold)
        for f in range(2):
            rows_all[a, e, half, :, pl.ds(f * fold, fold)] = dot(pack[e, f], got).astype(BF16)
        for copy in gather_copies(a, e):
            copy.start()

    def wait_gather(a, e):
        part = rows_all.at[a, e, pl.ds(0, n_half - 1)]
        pltpu.make_async_copy(part, part, ag_rs.at[2 * a + e]).wait()

    def project(w, a, e):
        total = jnp.zeros((hid, cap), F32)
        for h in range(n_half):
            total = total + dot(
                w_buf[w, e, :, pl.ds(h * quarter, quarter)], rows_all[a, e, h], ((1,), (1,))
            )
        return total

    def compute(e):
        wait_gather(0, e)
        pre_gate = project(0, 0, e)
        pre_up = project(1, 0, e)
        wait_gather(1, e)
        back = project(2, 1, e)
        sig = 1.0 / (1.0 + jnp.exp(-pre_gate))
        act = pre_gate * sig
        hidden = (act * pre_up).astype(BF16)
        d_gate = (back * pre_up * sig * (1.0 + pre_gate * (1.0 - sig))).astype(BF16)
        d_up = (back * act).astype(BF16)
        dg_r = jnp.transpose(d_gate)
        du_r = jnp.transpose(d_up)
        for i in (2, 1, 3, 0):
            to = lax.rem(half + i, n_half)
            cols = pl.ds(pl.multiple_of(to * quarter, quarter), quarter)
            value = dot(dg_r, w_buf[0, e, :, cols]) + dot(du_r, w_buf[1, e, :, cols])
            if i == 0:
                part_own[e] = value
            else:
                part_send[e, i - 1] = value.astype(BF16)
                pltpu.make_async_remote_copy(
                    src_ref=part_send.at[e, i - 1], dst_ref=part_recv.at[e, i - 1],
                    send_sem=rs_ss.at[e], recv_sem=rs_rs.at[e],
                    device_id={"half": to}, device_id_type=MESH,
                ).start()
        gg = jnp.sum(hidden.astype(F32) * back, axis=0, keepdims=True)
        gg_part[e] = jnp.broadcast_to(gg, (8, cap))
        for i in range(1, n_half):
            pltpu.make_async_remote_copy(
                src_ref=gg_part.at[e], dst_ref=gg_recv.at[e, i - 1],
                send_sem=ggx_ss.at[e], recv_sem=ggx_rs.at[e],
                device_id={"half": lax.rem(half + i, n_half)}, device_id_type=MESH,
            ).start()
        return hidden, d_gate, d_up

    def weight_grads(e, hidden, d_gate, d_up):
        for h in range(n_half):
            cols = pl.ds(h * quarter, quarter)
            x_h = rows_all[0, e, h]
            grads[0, e, :, cols] = dot(d_gate, x_h).astype(BF16)
            grads[1, e, :, cols] = dot(d_up, x_h).astype(BF16)
            grads[2, e, :, cols] = dot(hidden, rows_all[1, e, h]).astype(BF16)

    def send_home(e):
        pltpu.make_async_copy(part_send.at[e], part_recv.at[e], rs_rs.at[e]).wait()
        total = part_own[e]
        for i in range(n_half - 1):
            total = total + part_recv[e, i].astype(F32)
        block = folded(dot(spread[e], total.astype(BF16))).astype(BF16)
        ret_send[e] = block.reshape(n_src, 16, fold)
        send_all(ret_send.at[e], ret_recv.at[e], ret_ss.at[e], ret_rs.at[e])
        ret_recv[e, me] = ret_send[e, me]

    def gate_home():
        total = jnp.zeros((n_src, 128), F32)
        for e in range(2):
            pltpu.make_async_copy(gg_recv.at[e], gg_recv.at[e], ggx_rs.at[e]).wait()
            gg = gg_part[e]
            for i in range(n_half - 1):
                gg = gg + gg_recv[e, i]
            top = gg.astype(BF16).astype(F32)
            mid = (gg - top).astype(BF16).astype(F32)
            rest = gg - top - mid
            sub = iota((8, cap), 0)
            split = jnp.where(sub == 0, top, jnp.where(sub == 1, mid, jnp.where(sub == 2, rest, 0.0)))
            row = jnp.sum(dot(split.astype(BF16), pack[e, 0]), axis=0, keepdims=True)
            own = iota((n_src, slots), 1) // 16 == iota((n_src, slots), 0)
            spread_row = jnp.where(own, jnp.broadcast_to(row, (n_src, slots)), 0.0)
            col = iota((slots, 128), 0)
            to_lane = ((col // 8) % 2 == 0) & (iota((slots, 128), 1) == e * 8 + col % 8)
            total = total + dot(spread_row, to_lane.astype(F32), precision=lax.Precision.HIGHEST)
        ggh_send[...] = total.reshape(n_src, 1, 128)
        send_all(ggh_send, ggh_recv, ggh_ss, ggh_rs)
        ggh_recv[me] = ggh_send[me]

    take_in(0, 0)
    take_in(0, 1)
    take_in(1, 0)
    take_in(1, 1)
    for load in loads:
        load.wait()
    state0 = compute(0)
    state1 = compute(1)
    send_home(0)
    gate_home()
    weight_grads(0, *state0)
    send_home(1)
    weight_grads(1, *state1)
    stores = [
        pltpu.make_async_copy(grads.at[k], ref, grad_sem.at[k])
        for k, ref in enumerate((gwg_out, gwu_out, gwd_out))
    ]
    for store in stores:
        store.start()

    wait_all(ggh_recv, ggh_rs)
    got = ggh_recv[...].reshape(n_src, 128)
    gg_rows = jnp.zeros((experts, most), F32)
    for e in range(2):
        lanes = (iota((128, most), 0) == e * 8 + iota((128, most), 1)).astype(F32)
        place = (iota((experts, n_src), 0) == 2 * iota((experts, n_src), 1) + e).astype(F32)
        picked = dot(got, lanes, precision=lax.Precision.HIGHEST)
        gg_rows = gg_rows + dot(place, picked, precision=lax.Precision.HIGHEST)
    gg_out[...] = jnp.where(live, gg_rows / gates[...].astype(F32), 0.0).astype(BF16)

    wait_all(ret_recv.at[0], ret_rs.at[0])
    first = [dot(home_g[0, f], ret_recv[0].reshape(slots, fold)) for f in range(2)]
    wait_all(ret_recv.at[1], ret_rs.at[1])
    for f in range(2):
        last = first[f] + dot(home_g[1, f], ret_recv[1].reshape(slots, fold))
        gt_out[:, pl.ds(f * fold, fold)] = last.astype(BF16)

    wait_all(cnt_send, cnt_ss)
    wait_all(ggh_send, ggh_ss)
    for k in range(4):
        wait_all(fwd_send.at[k], fwd_ss.at[k])
    for a in range(2):
        for e in range(2):
            part = rows_all.at[a, e, pl.ds(0, n_half - 1)]
            pltpu.make_async_copy(part, part, ag_ss.at[2 * a + e]).wait()
    for e in range(2):
        pltpu.make_async_copy(part_send.at[e], part_send.at[e], rs_ss.at[e]).wait()
        pltpu.make_async_copy(gg_recv.at[e], gg_recv.at[e], ggx_ss.at[e]).wait()
        wait_all(ret_send.at[e], ret_ss.at[e])
    for store in stores:
        store.wait()


def body(n_src, n_half, tokens, out_grad, w_gate, w_up, w_down, chosen_rows, counts, gate_values):
    tok_dev, quarter = tokens.shape
    experts, _, most = chosen_rows.shape
    per, hid, width = w_gate.shape
    cap = 4 * n_src
    fold = quarter // 2
    vmem = pl.BlockSpec(memory_space=pltpu.VMEM)
    hbm = pl.BlockSpec(memory_space=pl.ANY)
    dma = pltpu.SemaphoreType.DMA
    grad_w = jax.ShapeDtypeStruct(w_gate.shape, BF16)
    outs = pl.pallas_call(
        functools.partial(kernel, n_src, n_half),
        out_shape=(
            jax.ShapeDtypeStruct(tokens.shape, BF16),
            grad_w, grad_w, grad_w,
            jax.ShapeDtypeStruct((experts, most), BF16),
        ),
        in_specs=[vmem] * 5 + [hbm] * 3,
        out_specs=(vmem, hbm, hbm, hbm, vmem),
        scratch_shapes=[
            pltpu.VMEM((3, per, hid, width), BF16),
            dma((3,)),
            pltpu.VMEM((n_src, 1, 128), F32),
            pltpu.VMEM((n_src, 1, 128), F32),
            pltpu.VMEM((4, n_src, 16, fold), BF16),
            pltpu.VMEM((4, n_src, 16, fold), BF16),
            pltpu.VMEM((2, 2, tok_dev, n_src * 16), BF16),
            pltpu.VMEM((2, 2, cap, n_src * 16), BF16),
            pltpu.VMEM((2, n_src * 16, cap), BF16),
            pltpu.VMEM((2, 2, n_half, cap, quarter), BF16),
            pltpu.VMEM((2, n_half - 1, cap, quarter), BF16),
            pltpu.VMEM((2, n_half - 1, cap, quarter), BF16),
            pltpu.VMEM((2, cap, quarter), F32),
            pltpu.VMEM((2, 8, cap), F32),
            pltpu.VMEM((2, n_half - 1, 8, cap), F32),
            pltpu.VMEM((n_src, 1, 128), F32),
            pltpu.VMEM((n_src, 1, 128), F32),
            pltpu.VMEM((2, n_src, 16, fold), BF16),
            pltpu.VMEM((2, n_src, 16, fold), BF16),
            pltpu.VMEM((3, per, hid, width), BF16),
            dma((3,)),
            dma, dma, dma((4,)), dma((4,)), dma((4,)), dma((4,)), dma((2,)), dma((2,)),
            dma((2,)), dma((2,)), dma((2,)), dma((2,)), dma, dma,
        ],
        compiler_params=pltpu.CompilerParams(
            collective_id=0, has_side_effects=True, vmem_limit_bytes=56 * 2**20
        ),
        cost_estimate=pl.CostEstimate(flops=4 * 10**9, bytes_accessed=10**7, transcendentals=10**5),
        name="experts_backward",
    )(
        tokens, out_grad,
        chosen_rows.reshape(experts, most), counts, gate_values.reshape(experts, most),
        w_gate, w_up, w_down,
    )
    return outs[:4] + (outs[4].reshape(experts, 1, most),)


def solution(mesh):
    return jax.shard_map(
        functools.partial(body, mesh.shape["expert"], mesh.shape["half"]),
        mesh=mesh,
        in_specs=(
            P("expert", "half"),
            P("expert", "half"),
            P("expert", "half", None),
            P("expert", "half", None),
            P("expert", "half", None),
            P(None, "expert", None),
            P(None, "expert"),
            P(None, "expert", None),
        ),
        out_specs=(
            P("expert", "half"),
            P("expert", "half", None),
            P("expert", "half", None),
            P("expert", "half", None),
            P(None, "expert", None),
        ),
        check_vma=False,
    )
```

time: 276 us -> 136 us (0.49)
  Pallas kernels: 0 us -> 121 us
  blocking collectives: 98.1 us -> 0 us
  waiting for transfers between devices: 89.1 us -> 0 us
  matrix products: 27.6 us -> 0 us
  starting transfers between devices: 23.9 us -> 0 us
  between operations: 13.9 us -> 0.65 us
  local copies, waits for them, and re-layouts: 19.9 us -> 13.2 us
  other arithmetic: 3.37 us -> 0 us
    pallas_call x0 -> x1, Pallas kernels: none -> 121 us  [body(): pl.pallas_call(functools.partial(kernel, n_src, n_half), out_shape=(jax.S...]
    all_to_all x3 -> x0, blocking collectives: 91.5 us -> none  [the longest x1 41.6 us: body(): lax.all_to_all(token_send, 'expert', split_axis=0, concat_axis=1, tiled=T...]
    all_gather x2 -> x0, waiting for transfers between devices: 41.3 us -> none  [the longest x1 41.3 us: body(): lax.all_gather(grad_recv, 'half', axis=2, tiled=True)]
    reduce_scatter x1 -> x0, waiting for transfers between devices: 29.6 us -> none  [body(): lax.psum_scatter(partial_value.astype(jnp.bfloat16), 'half', scatter_dime...]
    dot_general x9 -> x0, matrix products: 27.6 us -> none  [the longest x1 5.64 us: body(): jnp.einsum('erd,efd->erf', dy_rows, w_down, preferred_element_type=jnp.fl...]
    all_to_all x2 -> x0, starting transfers between devices: 23.8 us -> none  [the longest x1 13 us: body(): lax.all_to_all(gate_grad_rows, 'expert', split_axis=1, concat_axis=0, til...]
    all_to_all x2 -> x0, waiting for transfers between devices: 18.2 us -> none  [the longest x1 18.2 us: body(): lax.all_to_all(row_grad, 'expert', split_axis=1, concat_axis=0, tiled=True)]
    unnamed x30 -> x12, local copies, waits for them, and re-layouts: 2.92 us -> 13.2 us
  transfers between devices with their start and end apart: 5 -> 0, of which waited for: 3 -> 0; matrix products, arithmetic and copies ran while one was open for 9% -> 0% of each run, Pallas kernels for 0% -> 0%
where the time goes in v1:
time: 136 us; the launch traced here: 135 us
  Pallas kernels  121 us (89%)
  local copies, waits for them, and re-layouts  13.2 us (10%)
    pallas_call x1, Pallas kernels, body(): pl.pallas_call(functools.partial(kernel, n_src, n_half), out_shape=(jax.S...  121 us
    unnamed x12, local copies, waits for them, and re-layouts  13.2 us

profile of v1, /device:TPU:1, one launch (start us, length us, event | category | flops | bytes accessed | tf_op | source)
XLA Modules:
  0.0 135.4 jit_solution(18399194237920802880)
XLA Ops:
  0.6 1.4 %copy.14 = bf16[128,1,8]{2,0,1:T(8,128)(2,1)} copy(bf16[128,1,8]{0,2,1:T(8,128)(2,1)} %param.15) | data formatting | bytes 4096 | tf_op args[7]
  2.0 1.4 %copy.13 = s32[128,1,8]{2,0,1:T(8,128)} copy(s32[128,1,8]{0,2,1:T(8,128)} %param.13) | data formatting | bytes 8192 | tf_op args[5]
  3.4 1.4 %copy.15.counts = s32[128,1]{1,0:T(8,128)} copy(s32[128,1]{0,1:T(1,128)} %param.14) | data formatting | bytes 1024 | tf_op args[6]
  4.8 121.5 %experts_backward.1 = (bf16[256,512]{1,0:T(8,128)(2,1)}, bf16[2,192,2048]{2,1,0:T(8,128)(2,1)}, bf16[2,192,2048]{2,1,0:T(8,128)(2,1)}, bf16[2,192,2048]{2,1,0:T(8,128)(2,1)}, bf16[128,8]{1,0:T(8,128)(2,1)}) custom-call(bf16[256,512]{1,0:T(8,128)(2,1)} %tok.1, bf16[256,512]{1,0:T(8,128)(2,1)} %out_grad.1, s32[128,8]{1,0:T(8,128)} %bitcast.3, ...), custom_call_target="tpu_custom_call" | custom-call | flops 4000000000 | bytes 10000000 | tf_op jit(solution)/shard_map/experts_backward/pallas_call | solution.py:319
  126.3 1.4 %copy.16 = bf16[128,1,8]{0,2,1:T(8,128)(2,1)} copy(bf16[128,1,8]{2,0,1:T(8,128)(2,1)} %bitcast.4) | data formatting | bytes 4096
  127.7 1.7 %copy.21 = bf16[256,512]{1,0:T(8,128)(2,1)} copy(bf16[256,512]{1,0:T(8,128)(2,1)} %get-tuple-element.25) | data formatting | bytes 524288
  129.4 0.0 copy-start.1
  129.4 2.8 %copy.22 = bf16[2,192,2048]{2,1,0:T(8,128)(2,1)} copy(bf16[2,192,2048]{2,1,0:T(8,128)(2,1)} %get-tuple-element.26) | data formatting | bytes 3145728
  132.2 0.0 copy-done.1
  132.2 0.0 copy-start
  132.2 1.1 copy.23
  133.4 0.8 copy-done
  134.2 1.1 copy.24
Async XLA Ops:
  129.4 2.9 %copy-start.1 = (bf16[2,192,2048]{2,1,0:T(8,128)(2,1)S(1)}, bf16[2,192,2048]{2,1,0:T(8,128)(2,1)}, u32[]{:S(2)}) copy-start(bf16[2,192,2048]{2,1,0:T(8,128)(2,1)} %get-tuple-element.27) | copy-start | bytes 4718596
  132.2 2.0 %copy-start = (bf16[2,192,2048]{2,1,0:T(8,128)(2,1)S(1)}, bf16[2,192,2048]{2,1,0:T(8,128)(2,1)}, u32[]{:S(2)}) copy-start(bf16[2,192,2048]{2,1,0:T(8,128)(2,1)} %get-tuple-element.28) | copy-start | bytes 4718596

commit v2 on v0

v2 whole, which is shorter than its diff:
```python
import functools

import jax
import jax.numpy as jnp
from jax import lax
from jax.experimental import pallas as pl
from jax.experimental.pallas import tpu as pltpu
from jax.sharding import PartitionSpec as P

MESH = pl.DeviceIdType.MESH
F32, BF16 = jnp.float32, jnp.bfloat16
NT = ((1,), (1,))
PIECES = tuple((a, e, q) for e in range(2) for a in range(2) for q in range(2))


def iota(shape, dim):
    return lax.broadcasted_iota(jnp.int32, shape, dim)


def dot(a, b, dims=((1,), (0,)), precision=None):
    return lax.dot_general(a, b, (dims, ((), ())), preferred_element_type=F32, precision=precision)


def kernel(
    n_src, n_half,
    tok_hbm, out_grad_hbm, chosen_hbm, counts_hbm, gates_hbm, wg_hbm, wu_hbm, wd_hbm,
    gt_out, grads_g, grads_u, grads_d, gg_out,
    tok, out_grad, chosen, counts, gates, in_sem,
    w_buf, w_sem, hot_buf,
    cnt_send, cnt_recv, fwd_send, fwd_recv,
    home_g, pack, spread,
    rows_all, part_send, part_recv, part_own, keep,
    gg_part, gg_recv, ggh_send, ggh_recv,
    ret_send, ret_recv,
    cnt_ss, cnt_rs, fwd_ss, fwd_rs, ag_ss, ag_rs, rs_ss, rs_rs,
    ggx_ss, ggx_rs, ret_ss, ret_rs, ggh_ss, ggh_rs,
):
    me = lax.axis_index("expert")
    half = lax.axis_index("half")
    tokens = tok.shape[0]
    quarter = tok.shape[1]
    fold = quarter // 2
    lane = fold // 2
    slots = n_src * 16
    cap = rows_all.shape[4]
    mid = cap // 2
    hid = wg_hbm.shape[1]
    most, experts = chosen.shape
    piece_of = {piece: k for k, piece in enumerate(PIECES)}

    ins = [
        pltpu.make_async_copy(src, dst, in_sem.at[k])
        for k, (src, dst) in enumerate((
            (chosen_hbm, chosen), (counts_hbm, counts), (gates_hbm, gates), (tok_hbm, tok), (out_grad_hbm, out_grad)
        ))
    ]
    loads = [
        pltpu.make_async_copy(ref, w_buf.at[k], w_sem.at[k]) for k, ref in enumerate((wg_hbm, wu_hbm, wd_hbm))
    ]
    for copy in ins:
        copy.start()

    barrier = pltpu.get_barrier_semaphore()

    @pl.loop(1, n_src)
    def _(i):
        pl.semaphore_signal(barrier, inc=1, device_id={"expert": lax.rem(me + i, n_src)}, device_id_type=MESH)

    for i in range(1, n_half):
        pl.semaphore_signal(barrier, inc=1, device_id={"half": lax.rem(half + i, n_half)}, device_id_type=MESH)

    for copy in ins:
        copy.wait()
    for load in loads:
        load.start()

    live = iota((most, experts), 0) < counts[...]
    chosen_live = jnp.where(live, chosen[...], -1).astype(F32).astype(BF16)
    gates_live = jnp.where(live, gates[...].astype(F32), 0.0).astype(BF16)

    def send_all(src, dst, ss, rs):
        @pl.loop(1, n_src)
        def _(i):
            to = lax.rem(me + i, n_src)
            pltpu.make_async_remote_copy(
                src_ref=src.at[to], dst_ref=dst.at[me], send_sem=ss, recv_sem=rs,
                device_id={"expert": to}, device_id_type=MESH,
            ).start()

    def wait_for(buf, sem):
        pltpu.make_async_copy(buf, buf, sem).wait()

    def wait_all(buf, sem):
        wait_for(buf.at[pl.ds(0, n_src - 1)], sem)

    def folded(wide):
        low = (iota((slots, lane), 0) // 8) % 2 == 0
        return jnp.where(low, wide[:, :lane], wide[:, lane:]).astype(BF16).reshape(n_src, 16, lane)

    def spread_column(e, table):
        mine = (iota((slots, experts), 1) == 2 * (iota((slots, experts), 0) // 16) + e).astype(BF16)
        slot_j = iota((slots, most), 1) == iota((slots, most), 0) % 8
        picked = jnp.where(slot_j, dot(mine, table, NT), 0.0).astype(BF16)
        return dot(picked, jnp.ones((most, tokens), BF16))

    def pick(a, e):
        hot = spread_column(e, chosen_live) == iota((slots, tokens), 1).astype(F32)
        value = 1.0 if a == 0 else spread_column(e, gates_live)
        hot_buf[...] = jnp.where(hot, value, 0.0).astype(BF16)

    def fill(a, e, q):
        k = piece_of[a, e, q]
        src = tok if a == 0 else out_grad
        fwd_send[k] = folded(dot(hot_buf[...], src[:, pl.ds(q * fold, fold)]))
        fwd_recv[k, me] = fwd_send[k, me]

    def send_piece(k):
        send_all(fwd_send.at[k], fwd_recv.at[k], fwd_ss.at[k], fwd_rs.at[k])

    pick(0, 0)
    fill(0, 0, 0)
    pl.semaphore_wait(barrier, n_src - 1 + n_half - 1)
    send_piece(0)
    count_wide = jnp.broadcast_to(counts[...].astype(F32), (128, experts)).astype(BF16)
    rows_to = jnp.zeros((n_src, 128), F32)
    for e in range(2):
        mine = (iota((n_src, experts), 1) == 2 * iota((n_src, experts), 0) + e).astype(BF16)
        rows_to = rows_to + jnp.where(iota((n_src, 128), 1) == e, dot(mine, count_wide, NT), 0.0)
    cnt_send[...] = rows_to.reshape(n_src, 1, 128)
    cnt_recv[me] = cnt_send[me]
    send_all(cnt_send, cnt_recv, cnt_ss, cnt_rs)
    fill(0, 0, 1)
    send_piece(1)
    pick(1, 0)
    fill(1, 0, 0)
    send_piece(2)
    fill(1, 0, 1)
    send_piece(3)

    def make_pack(e):
        count_all = cnt_recv[...].reshape(n_src, 128).astype(BF16)
        by_col = dot(count_all, (iota((128, slots), 0) == e).astype(BF16))
        src_of = iota((n_src, slots), 1) // 16
        before = jnp.sum(jnp.where(iota((n_src, slots), 0) < src_of, by_col, 0.0), axis=0, keepdims=True)
        size = jnp.sum(jnp.where(iota((n_src, slots), 0) == src_of, by_col, 0.0), axis=0, keepdims=True)
        j = (iota((1, slots), 1) % 8).astype(F32)
        place = jnp.where(j < size, before + j, -1.0)
        hit = place == iota((cap, slots), 0).astype(F32)
        in_half = (iota((cap, slots), 1) // 8) % 2
        for g in range(2):
            pack[e, g] = jnp.where(hit & (in_half == g), 1.0, 0.0).astype(BF16)

    def make_spread(e):
        count_all = cnt_recv[...].reshape(n_src, 128).astype(BF16)
        own_wide = dot(count_all, (iota((128, cap), 0) == e).astype(BF16)).astype(BF16)
        src_row = iota((slots, n_src), 0) // 16
        before = dot((iota((slots, n_src), 1) < src_row).astype(BF16), own_wide)
        size = dot((iota((slots, n_src), 1) == src_row).astype(BF16), own_wide)
        j = (iota((slots, cap), 0) % 8).astype(F32)
        place = jnp.where(j < size, before + j, -1.0)
        spread[e] = jnp.where(place == iota((slots, cap), 1).astype(F32), 1.0, 0.0).astype(BF16)

    def make_home(e):
        in_half = (iota((tokens, slots), 1) // 8) % 2
        mine = (iota((experts, slots), 0) == 2 * (iota((experts, slots), 1) // 16) + e).astype(BF16)
        row = dot(chosen_live, mine)
        row = jnp.sum(jnp.where(iota((most, slots), 0) == iota((most, slots), 1) % 8, row, 0.0), axis=0, keepdims=True)
        hit = row == iota((tokens, slots), 0).astype(F32)
        for g in range(2):
            home_g[e, g] = jnp.where(hit & (in_half == g), 1.0, 0.0).astype(BF16)

    def to_half(src, dst, ss, rs, step):
        return pltpu.make_async_remote_copy(
            src_ref=src, dst_ref=dst, send_sem=ss, recv_sem=rs,
            device_id={"half": lax.rem(half + step, n_half)}, device_id_type=MESH,
        )

    low_rows, high_rows = pl.ds(0, mid), pl.ds(mid, mid)

    def take_in(a, e, q):
        k = piece_of[a, e, q]

        def pass_on(ref, n, step):
            to_half(ref, ref, ag_ss.at[k, n], ag_rs.at[k, n], step).start()

        wait_all(fwd_recv.at[k], fwd_rs.at[k])
        got = fwd_recv[k].reshape(slots, lane)
        for g in range(2):
            rows_all[a, e, q, half, :, pl.ds(g * lane, lane)] = dot(pack[e, g], got).astype(BF16)
        mine = rows_all.at[a, e, q, half]
        pass_on(mine.at[low_rows], 0, 1)
        pass_on(mine.at[high_rows], 1, 3)
        pass_on(mine.at[high_rows], 2, 1)
        pass_on(mine.at[low_rows], 3, 3)
        left = rows_all.at[a, e, q, lax.rem(half + 3, n_half), low_rows]
        right = rows_all.at[a, e, q, lax.rem(half + 1, n_half), high_rows]
        wait_for(left, ag_rs.at[k, 0])
        pass_on(left, 4, 1)
        wait_for(right, ag_rs.at[k, 1])
        pass_on(right, 5, 3)

    def wait_gather(a, e):
        for q in range(2):
            for n in (2, 3, 4, 5):
                wait_for(rows_all.at[a, e, q, 0, low_rows], ag_rs.at[piece_of[a, e, q], n])

    def project(w, a, e):
        total = jnp.zeros((hid, cap), F32)
        for h in range(n_half):
            for q in range(2):
                cols = pl.ds(h * quarter + q * fold, fold)
                total = total + dot(w_buf[w, e, :, cols], rows_all[a, e, q, h], NT)
        return total

    def forward(e):
        wait_gather(0, e)
        pre_gate = project(0, 0, e)
        pre_up = project(1, 0, e)
        sig = 1.0 / (1.0 + jnp.exp(-pre_gate))
        act = pre_gate * sig
        hidden = (act * pre_up).astype(BF16)
        slope = pre_up * sig * (1.0 + pre_gate * (1.0 - sig))
        return hidden, act, slope

    def backward(e, hidden, act, slope):
        wait_gather(1, e)
        back = project(2, 1, e)
        d_gate = (back * slope).astype(BF16)
        d_up = (back * act).astype(BF16)
        dg_r = jnp.transpose(d_gate)
        du_r = jnp.transpose(d_up)
        for q in range(2):
            s = 2 * e + q

            def value(step):
                to = lax.rem(half + step, n_half)
                cols = pl.ds(pl.multiple_of(to * quarter + q * fold, fold), fold)
                return dot(dg_r, w_buf[0, e, :, cols]) + dot(du_r, w_buf[1, e, :, cols])

            def push(n, block, step):
                part_send[s, n] = block.astype(BF16)
                to_half(part_send.at[s, n], part_recv.at[s, n], rs_ss.at[s, n], rs_rs.at[s, n], step).start()

            far = value(2)
            push(0, far[:mid], 1)
            push(1, far[mid:], 3)
            right = value(1)
            push(2, right[mid:], 1)
            keep[s, 0] = right[:mid]
            left = value(3)
            push(3, left[:mid], 3)
            keep[s, 1] = left[mid:]
            part_own[s] = value(0)
        gg = jnp.sum(hidden.astype(F32) * back, axis=0, keepdims=True)
        gg_part[e] = jnp.broadcast_to(gg, (8, cap))
        for i in range(1, n_half):
            to_half(gg_part.at[e], gg_recv.at[e, i - 1], ggx_ss.at[e], ggx_rs.at[e], i).start()
        return d_gate, d_up

    def relay(e):
        for q in range(2):
            s = 2 * e + q
            for n, step in ((0, 1), (1, 3)):
                wait_for(part_recv.at[s, n], rs_rs.at[s, n])
                part_send[s, 4 + n] = (keep[s, n] + part_recv[s, n].astype(F32)).astype(BF16)
                to_half(
                    part_send.at[s, 4 + n], part_recv.at[s, 4 + n], rs_ss.at[s, 4 + n], rs_rs.at[s, 4 + n], step
                ).start()

    def weight_grads(e, hidden, d_gate, d_up):
        for h in range(n_half):
            for q in range(2):
                cols = pl.ds(h * quarter + q * fold, fold)
                x_h = rows_all[0, e, q, h]
                grads_g[e, :, cols] = dot(d_gate, x_h).astype(BF16)
                grads_u[e, :, cols] = dot(d_up, x_h).astype(BF16)
                grads_d[e, :, cols] = dot(hidden, rows_all[1, e, q, h]).astype(BF16)

    def send_home(e, q):
        s = 2 * e + q
        for n in (2, 3, 4, 5):
            wait_for(part_recv.at[s, n], rs_rs.at[s, n])
        low = part_own[s, low_rows] + part_recv[s, 4].astype(F32) + part_recv[s, 3].astype(F32)
        high = part_own[s, high_rows] + part_recv[s, 2].astype(F32) + part_recv[s, 5].astype(F32)
        total = jnp.concatenate([low.astype(BF16), high.astype(BF16)], axis=0)
        ret_send[s] = folded(dot(spread[e], total))
        ret_recv[s, me] = ret_send[s, me]
        send_all(ret_send.at[s], ret_recv.at[s], ret_ss.at[s], ret_rs.at[s])

    def gate_home():
        total = jnp.zeros((n_src, 128), F32)
        for e in range(2):
            wait_for(gg_recv.at[e], ggx_rs.at[e])
            gg = gg_part[e]
            for i in range(n_half - 1):
                gg = gg + gg_recv[e, i]
            top = gg.astype(BF16).astype(F32)
            mid_part = (gg - top).astype(BF16).astype(F32)
            rest = gg - top - mid_part
            sub = iota((8, cap), 0)
            split = jnp.where(sub == 0, top, jnp.where(sub == 1, mid_part, jnp.where(sub == 2, rest, 0.0)))
            row = jnp.sum(dot(split.astype(BF16), pack[e, 0]), axis=0, keepdims=True)
            own = iota((n_src, slots), 1) // 16 == iota((n_src, slots), 0)
            spread_row = jnp.where(own, jnp.broadcast_to(row, (n_src, slots)), 0.0)
            col = iota((slots, 128), 0)
            to_lane = ((col // 8) % 2 == 0) & (iota((slots, 128), 1) == e * 8 + col % 8)
            total = total + dot(spread_row, to_lane.astype(F32), precision=lax.Precision.HIGHEST)
        ggh_send[...] = total.reshape(n_src, 1, 128)
        ggh_recv[me] = ggh_send[me]
        send_all(ggh_send, ggh_recv, ggh_ss, ggh_rs)

    wait_all(cnt_recv, cnt_rs)
    make_pack(0)
    take_in(*PIECES[0])
    pick(0, 1)
    fill(0, 1, 0)
    send_piece(4)
    take_in(*PIECES[1])
    fill(0, 1, 1)
    send_piece(5)
    for load in loads:
        load.wait()
    take_in(*PIECES[2])
    pick(1, 1)
    fill(1, 1, 0)
    send_piece(6)
    fwd0 = forward(0)
    take_in(*PIECES[3])
    fill(1, 1, 1)
    send_piece(7)
    make_pack(1)
    take_in(*PIECES[4])
    back0 = backward(0, *fwd0)
    make_spread(0)
    take_in(*PIECES[5])
    relay(0)
    make_spread(1)
    take_in(*PIECES[6])
    fwd1 = forward(1)
    make_home(0)
    take_in(*PIECES[7])
    send_home(0, 0)
    send_home(0, 1)
    back1 = backward(1, *fwd1)
    weight_grads(0, fwd0[0], *back0)
    relay(1)
    gate_home()
    make_home(1)
    send_home(1, 0)
    send_home(1, 1)
    weight_grads(1, fwd1[0], *back1)

    wait_all(ggh_recv, ggh_rs)
    got = ggh_recv[...].reshape(n_src, 128)
    gg_rows = jnp.zeros((most, experts), F32)
    for e in range(2):
        lanes = (iota((most, 128), 1) == e * 8 + iota((most, 128), 0)).astype(F32)
        place = (iota((n_src, experts), 1) == 2 * iota((n_src, experts), 0) + e).astype(F32)
        picked = dot(lanes, got, NT, precision=lax.Precision.HIGHEST)
        gg_rows = gg_rows + dot(picked, place, precision=lax.Precision.HIGHEST)
    gg_out[...] = jnp.where(live, gg_rows / gates[...].astype(F32), 0.0).astype(BF16)

    def home_sum(s):
        wait_all(ret_recv.at[s], ret_rs.at[s])
        got = ret_recv[s].reshape(slots, lane)
        return [dot(home_g[s // 2, g], got) for g in range(2)]

    first = [home_sum(0), home_sum(1)]
    for q in range(2):
        last = home_sum(2 + q)
        for g in range(2):
            gt_out[:, pl.ds(q * fold + g * lane, lane)] = (first[q][g] + last[g]).astype(BF16)

    wait_all(cnt_send, cnt_ss)
    wait_all(ggh_send, ggh_ss)
    for k, (a, e, q) in enumerate(PIECES):
        wait_all(fwd_send.at[k], fwd_ss.at[k])
        for n in range(6):
            wait_for(rows_all.at[a, e, q, 0, low_rows], ag_ss.at[k, n])
    for s in range(4):
        wait_all(ret_send.at[s], ret_ss.at[s])
        for n in range(6):
            wait_for(part_send.at[s, n], rs_ss.at[s, n])
    for e in range(2):
        wait_for(gg_recv.at[e], ggx_ss.at[e])


def write_out(a, b, c, d, e, ao, bo, co, do, eo, sem):
    copies = [
        pltpu.make_async_copy(src, dst, sem.at[k])
        for k, (src, dst) in enumerate(((b, bo), (c, co), (d, do), (a, ao), (e, eo)))
    ]
    for copy in copies:
        copy.start()
    for copy in copies:
        copy.wait()


def body(n_src, n_half, tokens, out_grad, w_gate, w_up, w_down, chosen_rows, counts, gate_values):
    tok_dev, quarter = tokens.shape
    experts, _, most = chosen_rows.shape
    per, hid, width = w_gate.shape
    cap = 4 * n_src
    fold = quarter // 2
    lane = fold // 2
    slots = n_src * 16
    vmem = pl.BlockSpec(memory_space=pltpu.VMEM)
    hbm = pl.BlockSpec(memory_space=pltpu.HBM)
    dma = pltpu.SemaphoreType.DMA
    grad_w = jax.ShapeDtypeStruct(w_gate.shape, BF16)
    shapes = (
        jax.ShapeDtypeStruct(tokens.shape, BF16),
        grad_w, grad_w, grad_w,
        jax.ShapeDtypeStruct((most, experts), BF16),
    )
    args = (
        tokens, out_grad,
        chosen_rows.reshape(experts, most).T, counts.T, gate_values.reshape(experts, most).T,
        w_gate, w_up, w_down,
    )
    outs = pl.pallas_call(
        functools.partial(kernel, n_src, n_half),
        out_shape=tuple(pltpu.VMEM(s.shape, s.dtype) for s in shapes),
        in_specs=[hbm] * 8,
        out_specs=(vmem,) * 5,
        scratch_shapes=[
            pltpu.VMEM(tokens.shape, BF16),
            pltpu.VMEM(tokens.shape, BF16),
            pltpu.VMEM((most, experts), jnp.int32),
            pltpu.VMEM((1, experts), jnp.int32),
            pltpu.VMEM((most, experts), BF16),
            dma((5,)),
            pltpu.VMEM((3, per, hid, width), BF16),
            dma((3,)),
            pltpu.VMEM((slots, tok_dev), BF16),
            pltpu.VMEM((n_src, 1, 128), F32),
            pltpu.VMEM((n_src, 1, 128), F32),
            pltpu.VMEM((8, n_src, 16, lane), BF16),
            pltpu.VMEM((8, n_src, 16, lane), BF16),
            pltpu.VMEM((2, 2, tok_dev, slots), BF16),
            pltpu.VMEM((2, 2, cap, slots), BF16),
            pltpu.VMEM((2, slots, cap), BF16),
            pltpu.VMEM((2, 2, 2, n_half, cap, fold), BF16),
            pltpu.VMEM((4, 6, cap // 2, fold), BF16),
            pltpu.VMEM((4, 6, cap // 2, fold), BF16),
            pltpu.VMEM((4, cap, fold), F32),
            pltpu.VMEM((4, 2, cap // 2, fold), F32),
            pltpu.VMEM((2, 8, cap), F32),
            pltpu.VMEM((2, n_half - 1, 8, cap), F32),
            pltpu.VMEM((n_src, 1, 128), F32),
            pltpu.VMEM((n_src, 1, 128), F32),
            pltpu.VMEM((4, n_src, 16, lane), BF16),
            pltpu.VMEM((4, n_src, 16, lane), BF16),
            dma, dma, dma((8,)), dma((8,)), dma((8, 6)), dma((8, 6)), dma((4, 6)), dma((4, 6)),
            dma((2,)), dma((2,)), dma((4,)), dma((4,)), dma, dma,
        ],
        compiler_params=pltpu.CompilerParams(
            collective_id=0, has_side_effects=True, vmem_limit_bytes=46 * 2**20
        ),
        cost_estimate=pl.CostEstimate(flops=4 * 10**9, bytes_accessed=10**7, transcendentals=10**5),
        name="experts_backward",
    )(*(pltpu.with_memory_space_constraint(a, pltpu.HBM) for a in args))
    outs = pl.pallas_call(
        write_out,
        out_shape=shapes,
        in_specs=[pl.BlockSpec(memory_space=pl.ANY)] * 5,
        out_specs=(hbm,) * 5,
        scratch_shapes=[dma((5,))],
        compiler_params=pltpu.CompilerParams(vmem_limit_bytes=2**20),
        name="write_out",
    )(*outs)
    return outs[:4] + (outs[4].T.reshape(experts, 1, most),)


def solution(mesh):
    return jax.shard_map(
        functools.partial(body, mesh.shape["expert"], mesh.shape["half"]),
        mesh=mesh,
        in_specs=(
            P("expert", "half"),
            P("expert", "half"),
            P("expert", "half", None),
            P("expert", "half", None),
            P("expert", "half", None),
            P(None, "expert", None),
            P(None, "expert"),
            P(None, "expert", None),
        ),
        out_specs=(
            P("expert", "half"),
            P("expert", "half", None),
            P("expert", "half", None),
            P("expert", "half", None),
            P(None, "expert", None),
        ),
        check_vma=False,
    )
```

time: 276 us -> 109 us (0.39)
  Pallas kernels: 0 us -> 108 us
  blocking collectives: 98.1 us -> 0 us
  waiting for transfers between devices: 89.1 us -> 0 us
  matrix products: 27.6 us -> 0 us
  starting transfers between devices: 23.9 us -> 0 us
  local copies, waits for them, and re-layouts: 19.9 us -> 0 us
  between operations: 13.9 us -> 0.8 us
  other arithmetic: 3.37 us -> 0 us
    pallas_call x0 -> x2, Pallas kernels: none -> 108 us  [the longest x1 106 us: body(): pl.pallas_call(functools.partial(kernel, n_src, n_half), out_shape=tuple(...]
    all_to_all x3 -> x0, blocking collectives: 91.5 us -> none  [the longest x1 41.6 us: body(): lax.all_to_all(token_send, 'expert', split_axis=0, concat_axis=1, tiled=T...]
    all_gather x2 -> x0, waiting for transfers between devices: 41.3 us -> none  [the longest x1 41.3 us: body(): lax.all_gather(grad_recv, 'half', axis=2, tiled=True)]
    reduce_scatter x1 -> x0, waiting for transfers between devices: 29.6 us -> none  [body(): lax.psum_scatter(partial_value.astype(jnp.bfloat16), 'half', scatter_dime...]
    dot_general x9 -> x0, matrix products: 27.6 us -> none  [the longest x1 5.64 us: body(): jnp.einsum('erd,efd->erf', dy_rows, w_down, preferred_element_type=jnp.fl...]
    all_to_all x2 -> x0, starting transfers between devices: 23.8 us -> none  [the longest x1 13 us: body(): lax.all_to_all(gate_grad_rows, 'expert', split_axis=1, concat_axis=0, til...]
    all_to_all x2 -> x0, waiting for transfers between devices: 18.2 us -> none  [the longest x1 18.2 us: body(): lax.all_to_all(row_grad, 'expert', split_axis=1, concat_axis=0, tiled=True)]
    gather x2 -> x0, local copies, waits for them, and re-layouts: 10.1 us -> none  [the longest x1 5.08 us: body(): jnp.take(out_grad, slots_flat, axis=0).reshape(experts, slot_most, quarter)]
  transfers between devices with their start and end apart: 5 -> 0, of which waited for: 3 -> 0; matrix products, arithmetic and copies ran while one was open for 9% -> 0% of each run, Pallas kernels for 0% -> 0%
where the time goes in v2:
time: 109 us
  Pallas kernels  108 us (99%)
    pallas_call x1, Pallas kernels, body(): pl.pallas_call(functools.partial(kernel, n_src, n_half), out_shape=tuple(...  106 us
    pallas_call x1, Pallas kernels, body(): pl.pallas_call(write_out, out_shape=shapes, in_specs=[pl.BlockSpec(memory...  2.3 us

profile of v2, /device:TPU:1, one launch (start us, length us, event | category | flops | bytes accessed | tf_op | source)
XLA Modules:
  0.0 109.0 jit_solution(1810332548851585533)
XLA Ops:
  0.6 105.9 %experts_backward.1 = (bf16[256,512]{1,0:T(8,128)(2,1)S(1)}, bf16[2,192,2048]{2,1,0:T(8,128)(2,1)S(1)}, bf16[2,192,2048]{2,1,0:T(8,128)(2,1)S(1)}, bf16[2,192,2048]{2,1,0:T(8,128)(2,1)S(1)}, bf16[8,128]{1,0:T(8,128)(2,1)S(1)}) custom-call(bf16[256,512]{1,0:T(8,128)(2,1)} %tok_hbm.1, bf16[256,512]{1,0:T(8,128)(2,1)} %out_grad_hbm.1, s32[8,128]{1,0:T(8,128)} %bitcast.10, ...), custom_call_target="tpu_custom_call" | custom-call | flops 4000000000 | bytes 10000000 | tf_op jit(solution)/shard_map/experts_backward/pallas_call | solution.py:421
  106.6 2.3 %write_out.1 = (bf16[256,512]{1,0:T(8,128)(2,1)}, bf16[2,192,2048]{2,1,0:T(8,128)(2,1)}, bf16[2,192,2048]{2,1,0:T(8,128)(2,1)}, bf16[2,192,2048]{2,1,0:T(8,128)(2,1)}, bf16[8,128]{1,0:T(8,128)(2,1)}) custom-call(bf16[256,512]{1,0:T(8,128)(2,1)S(1)} %get-tuple-element.15.a, bf16[2,192,2048]{2,1,0:T(8,128)(2,1)S(1)} %get-tuple-element.16.b, ...), custom_call_target="tpu_custom_call" | custom-call | tf_op jit(solution)/shard_map/write_out/pallas_call | solution.py:463

commit v3 on v2

--- a/solution.py
+++ b/solution.py
@@ -117,8 +117,17 @@
     def send_piece(k):
         send_all(fwd_send.at[k], fwd_recv.at[k], fwd_ss.at[k], fwd_rs.at[k])
 
-    pick(0, 0)
-    fill(0, 0, 0)
+    ahead = 3
+
+    def prep(k):
+        if k >= len(PIECES):
+            return
+        a, e, q = PIECES[k]
+        if q == 0:
+            pick(a, e)
+        fill(a, e, q)
+
+    prep(0)
     pl.semaphore_wait(barrier, n_src - 1 + n_half - 1)
     send_piece(0)
     count_wide = jnp.broadcast_to(counts[...].astype(F32), (128, experts)).astype(BF16)
@@ -129,13 +138,10 @@
     cnt_send[...] = rows_to.reshape(n_src, 1, 128)
     cnt_recv[me] = cnt_send[me]
     send_all(cnt_send, cnt_recv, cnt_ss, cnt_rs)
-    fill(0, 0, 1)
-    send_piece(1)
-    pick(1, 0)
-    fill(1, 0, 0)
-    send_piece(2)
-    fill(1, 0, 1)
-    send_piece(3)
+    for k in range(1, ahead):
+        prep(k)
+        send_piece(k)
+    prep(ahead)
 
     def make_pack(e):
         count_all = cnt_recv[...].reshape(n_src, 128).astype(BF16)
@@ -192,6 +198,9 @@
         pass_on(mine.at[high_rows], 1, 3)
         pass_on(mine.at[high_rows], 2, 1)
         pass_on(mine.at[low_rows], 3, 3)
+        if k + ahead < len(PIECES):
+            send_piece(k + ahead)
+            prep(k + ahead + 1)
         left = rows_all.at[a, e, q, lax.rem(half + 3, n_half), low_rows]
         right = rows_all.at[a, e, q, lax.rem(half + 1, n_half), high_rows]
         wait_for(left, ag_rs.at[k, 0])
@@ -222,50 +231,54 @@
         slope = pre_up * sig * (1.0 + pre_gate * (1.0 - sig))
         return hidden, act, slope
 
+    def row_block(e, q, step, dg_r, du_r):
+        to = lax.rem(half + step, n_half)
+        cols = pl.ds(pl.multiple_of(to * quarter + q * fold, fold), fold)
+        return dot(dg_r, w_buf[0, e, :, cols]) + dot(du_r, w_buf[1, e, :, cols])
+
+    def push(s, n, block, step):
+        part_send[s, n] = block.astype(BF16)
+        to_half(part_send.at[s, n], part_recv.at[s, n], rs_ss.at[s, n], rs_rs.at[s, n], step).start()
+
+    def push_far(e, q, *rows):
+        s = 2 * e + q
+        far = row_block(e, q, 2, *rows)
+        push(s, 0, far[:mid], 1)
+        push(s, 1, far[mid:], 3)
+
+    def push_near(e, q, *rows):
+        s = 2 * e + q
+        right = row_block(e, q, 1, *rows)
+        push(s, 2, right[mid:], 1)
+        keep[s, 0] = right[:mid]
+        left = row_block(e, q, 3, *rows)
+        push(s, 3, left[:mid], 3)
+        keep[s, 1] = left[mid:]
+
+    def relay(e, q):
+        s = 2 * e + q
+        for n, step in ((0, 1), (1, 3)):
+            wait_for(part_recv.at[s, n], rs_rs.at[s, n])
+            push(s, 4 + n, keep[s, n] + part_recv[s, n].astype(F32), step)
+
     def backward(e, hidden, act, slope):
         wait_gather(1, e)
         back = project(2, 1, e)
         d_gate = (back * slope).astype(BF16)
         d_up = (back * act).astype(BF16)
-        dg_r = jnp.transpose(d_gate)
-        du_r = jnp.transpose(d_up)
-        for q in range(2):
-            s = 2 * e + q
-
-            def value(step):
-                to = lax.rem(half + step, n_half)
-                cols = pl.ds(pl.multiple_of(to * quarter + q * fold, fold), fold)
-                return dot(dg_r, w_buf[0, e, :, cols]) + dot(du_r, w_buf[1, e, :, cols])
-
-            def push(n, block, step):
-                part_send[s, n] = block.astype(BF16)
-                to_half(part_send.at[s, n], part_recv.at[s, n], rs_ss.at[s, n], rs_rs.at[s, n], step).start()
-
-            far = value(2)
-            push(0, far[:mid], 1)
-            push(1, far[mid:], 3)
-            right = value(1)
-            push(2, right[mid:], 1)
-            keep[s, 0] = right[:mid]
-            left = value(3)
-            push(3, left[:mid], 3)
-            keep[s, 1] = left[mid:]
-            part_own[s] = value(0)
+        rows = jnp.transpose(d_gate), jnp.transpose(d_up)
+        push_far(e, 0, *rows)
+        push_near(e, 0, *rows)
+        push_far(e, 1, *rows)
         gg = jnp.sum(hidden.astype(F32) * back, axis=0, keepdims=True)
         gg_part[e] = jnp.broadcast_to(gg, (8, cap))
         for i in range(1, n_half):
             to_half(gg_part.at[e], gg_recv.at[e, i - 1], ggx_ss.at[e], ggx_rs.at[e], i).start()
+        for q in range(2):
+            part_own[2 * e + q] = row_block(e, q, 0, *rows)
+        relay(e, 0)
+        push_near(e, 1, *rows)
         return d_gate, d_up
-
-    def relay(e):
-        for q in range(2):
-            s = 2 * e + q
-            for n, step in ((0, 1), (1, 3)):
-                wait_for(part_recv.at[s, n], rs_rs.at[s, n])
-                part_send[s, 4 + n] = (keep[s, n] + part_recv[s, n].astype(F32)).astype(BF16)
-                to_half(
-                    part_send.at[s, 4 + n], part_recv.at[s, 4 + n], rs_ss.at[s, 4 + n], rs_rs.at[s, 4 + n], step
-                ).start()
 
     def weight_grads(e, hidden, d_gate, d_up):
         for h in range(n_half):
@@ -312,40 +325,30 @@
     wait_all(cnt_recv, cnt_rs)
     make_pack(0)
     take_in(*PIECES[0])
-    pick(0, 1)
-    fill(0, 1, 0)
-    send_piece(4)
-    take_in(*PIECES[1])
-    fill(0, 1, 1)
-    send_piece(5)
     for load in loads:
         load.wait()
+    make_home(0)
+    take_in(*PIECES[1])
+    make_home(1)
     take_in(*PIECES[2])
-    pick(1, 1)
-    fill(1, 1, 0)
-    send_piece(6)
     fwd0 = forward(0)
+    make_pack(1)
     take_in(*PIECES[3])
-    fill(1, 1, 1)
-    send_piece(7)
-    make_pack(1)
+    make_spread(0)
     take_in(*PIECES[4])
     back0 = backward(0, *fwd0)
-    make_spread(0)
+    relay(0, 1)
     take_in(*PIECES[5])
-    relay(0)
     make_spread(1)
+    weight_grads(0, fwd0[0], *back0)
     take_in(*PIECES[6])
     fwd1 = forward(1)
-    make_home(0)
     take_in(*PIECES[7])
     send_home(0, 0)
     send_home(0, 1)
     back1 = backward(1, *fwd1)
-    weight_grads(0, fwd0[0], *back0)
-    relay(1)
+    relay(1, 1)
     gate_home()
-    make_home(1)
     send_home(1, 0)
     send_home(1, 1)
     weight_grads(1, fwd1[0], *back1)
@@ -360,17 +363,6 @@
         gg_rows = gg_rows + dot(picked, place, precision=lax.Precision.HIGHEST)
     gg_out[...] = jnp.where(live, gg_rows / gates[...].astype(F32), 0.0).astype(BF16)
 
-    def home_sum(s):
-        wait_all(ret_recv.at[s], ret_rs.at[s])
-        got = ret_recv[s].reshape(slots, lane)
-        return [dot(home_g[s // 2, g], got) for g in range(2)]
-
-    first = [home_sum(0), home_sum(1)]
-    for q in range(2):
-        last = home_sum(2 + q)
-        for g in range(2):
-            gt_out[:, pl.ds(q * fold + g * lane, lane)] = (first[q][g] + last[g]).astype(BF16)
-
     wait_all(cnt_send, cnt_ss)
     wait_all(ggh_send, ggh_ss)
     for k, (a, e, q) in enumerate(PIECES):
@@ -378,11 +370,24 @@
         for n in range(6):
             wait_for(rows_all.at[a, e, q, 0, low_rows], ag_ss.at[k, n])
     for s in range(4):
-        wait_all(ret_send.at[s], ret_ss.at[s])
         for n in range(6):
             wait_for(part_send.at[s, n], rs_ss.at[s, n])
     for e in range(2):
         wait_for(gg_recv.at[e], ggx_ss.at[e])
+
+    def home_sum(s):
+        wait_all(ret_recv.at[s], ret_rs.at[s])
+        got = ret_recv[s].reshape(slots, lane)
+        return [dot(home_g[s // 2, g], got) for g in range(2)]
+
+    first = [home_sum(0), home_sum(1)]
+    for q in range(2):
+        last = home_sum(2 + q)
+        for g in range(2):
+            gt_out[:, pl.ds(q * fold + g * lane, lane)] = (first[q][g] + last[g]).astype(BF16)
+
+    for s in range(4):
+        wait_all(ret_send.at[s], ret_ss.at[s])
 
 
 def write_out(a, b, c, d, e, ao, bo, co, do, eo, sem):

time: 109 us -> 106 us (0.972)
  Pallas kernels: 108 us -> 105 us
    pallas_call x1, Pallas kernels: 106 us -> 102 us  [body(): pl.pallas_call(functools.partial(kernel, n_src, n_half), out_shape=tuple(...]
where the time goes in v3:
time: 106 us; the launch traced here: 105 us
  Pallas kernels  105 us (99%)
    pallas_call x1, Pallas kernels, body(): pl.pallas_call(functools.partial(kernel, n_src, n_half), out_shape=tuple(...  102 us
    pallas_call x1, Pallas kernels, body(): pl.pallas_call(write_out, out_shape=shapes, in_specs=[pl.BlockSpec(memory...  2.3 us

profile of v3, /device:TPU:1, one launch (start us, length us, event | category | flops | bytes accessed | tf_op | source)
XLA Modules:
  0.0 105.5 jit_solution(11164638185064159331)
XLA Ops:
  0.6 102.4 %experts_backward.1 = (bf16[256,512]{1,0:T(8,128)(2,1)S(1)}, bf16[2,192,2048]{2,1,0:T(8,128)(2,1)S(1)}, bf16[2,192,2048]{2,1,0:T(8,128)(2,1)S(1)}, bf16[2,192,2048]{2,1,0:T(8,128)(2,1)S(1)}, bf16[8,128]{1,0:T(8,128)(2,1)S(1)}) custom-call(bf16[256,512]{1,0:T(8,128)(2,1)} %tok_hbm.1, bf16[256,512]{1,0:T(8,128)(2,1)} %out_grad_hbm.1, s32[8,128]{1,0:T(8,128)} %bitcast.10, ...), custom_call_target="tpu_custom_call" | custom-call | flops 4000000000 | bytes 10000000 | tf_op jit(solution)/shard_map/experts_backward/pallas_call | solution.py:426
  103.0 2.3 %write_out.1 = (bf16[256,512]{1,0:T(8,128)(2,1)}, bf16[2,192,2048]{2,1,0:T(8,128)(2,1)}, bf16[2,192,2048]{2,1,0:T(8,128)(2,1)}, bf16[2,192,2048]{2,1,0:T(8,128)(2,1)}, bf16[8,128]{1,0:T(8,128)(2,1)}) custom-call(bf16[256,512]{1,0:T(8,128)(2,1)S(1)} %get-tuple-element.15.a, bf16[2,192,2048]{2,1,0:T(8,128)(2,1)S(1)} %get-tuple-element.16.b, ...), custom_call_target="tpu_custom_call" | custom-call | tf_op jit(solution)/shard_map/write_out/pallas_call | solution.py:468

commit v4 on v3

--- a/solution.py
+++ b/solution.py
@@ -62,9 +62,10 @@
 
     barrier = pltpu.get_barrier_semaphore()
 
-    @pl.loop(1, n_src)
-    def _(i):
-        pl.semaphore_signal(barrier, inc=1, device_id={"expert": lax.rem(me + i, n_src)}, device_id_type=MESH)
+    for start, stop in ((n_src // 2, n_src), (1, n_src // 2)):
+        @pl.loop(start, stop)
+        def _(i):
+            pl.semaphore_signal(barrier, inc=1, device_id={"expert": lax.rem(me + i, n_src)}, device_id_type=MESH)
 
     for i in range(1, n_half):
         pl.semaphore_signal(barrier, inc=1, device_id={"half": lax.rem(half + i, n_half)}, device_id_type=MESH)
@@ -183,30 +184,31 @@
 
     low_rows, high_rows = pl.ds(0, mid), pl.ds(mid, mid)
 
+    def pass_on(k, ref, n, step):
+        to_half(ref, ref, ag_ss.at[k, n], ag_rs.at[k, n], step).start()
+
     def take_in(a, e, q):
         k = piece_of[a, e, q]
-
-        def pass_on(ref, n, step):
-            to_half(ref, ref, ag_ss.at[k, n], ag_rs.at[k, n], step).start()
-
         wait_all(fwd_recv.at[k], fwd_rs.at[k])
         got = fwd_recv[k].reshape(slots, lane)
         for g in range(2):
             rows_all[a, e, q, half, :, pl.ds(g * lane, lane)] = dot(pack[e, g], got).astype(BF16)
         mine = rows_all.at[a, e, q, half]
-        pass_on(mine.at[low_rows], 0, 1)
-        pass_on(mine.at[high_rows], 1, 3)
-        pass_on(mine.at[high_rows], 2, 1)
-        pass_on(mine.at[low_rows], 3, 3)
+        pass_on(k, mine.at[low_rows], 0, 1)
+        pass_on(k, mine.at[high_rows], 1, 3)
+        pass_on(k, mine.at[high_rows], 2, 1)
+        pass_on(k, mine.at[low_rows], 3, 3)
         if k + ahead < len(PIECES):
             send_piece(k + ahead)
             prep(k + ahead + 1)
+    def hand_on(a, e, q):
+        k = piece_of[a, e, q]
         left = rows_all.at[a, e, q, lax.rem(half + 3, n_half), low_rows]
         right = rows_all.at[a, e, q, lax.rem(half + 1, n_half), high_rows]
         wait_for(left, ag_rs.at[k, 0])
-        pass_on(left, 4, 1)
+        pass_on(k, left, 4, 1)
         wait_for(right, ag_rs.at[k, 1])
-        pass_on(right, 5, 3)
+        pass_on(k, right, 5, 3)
 
     def wait_gather(a, e):
         for q in range(2):
@@ -276,9 +278,12 @@
             to_half(gg_part.at[e], gg_recv.at[e, i - 1], ggx_ss.at[e], ggx_rs.at[e], i).start()
         for q in range(2):
             part_own[2 * e + q] = row_block(e, q, 0, *rows)
+        return d_gate, d_up, rows
+
+    def reduce_rest(e, rows):
         relay(e, 0)
         push_near(e, 1, *rows)
-        return d_gate, d_up
+        relay(e, 1)
 
     def weight_grads(e, hidden, d_gate, d_up):
         for h in range(n_half):
@@ -327,29 +332,37 @@
     take_in(*PIECES[0])
     for load in loads:
         load.wait()
+    hand_on(*PIECES[0])
     make_home(0)
     take_in(*PIECES[1])
+    hand_on(*PIECES[1])
     make_home(1)
     take_in(*PIECES[2])
+    hand_on(*PIECES[2])
     fwd0 = forward(0)
     make_pack(1)
     take_in(*PIECES[3])
+    hand_on(*PIECES[3])
     make_spread(0)
     take_in(*PIECES[4])
-    back0 = backward(0, *fwd0)
-    relay(0, 1)
+    *back0, rows0 = backward(0, *fwd0)
+    hand_on(*PIECES[4])
+    reduce_rest(0, rows0)
     take_in(*PIECES[5])
     make_spread(1)
+    hand_on(*PIECES[5])
     weight_grads(0, fwd0[0], *back0)
     take_in(*PIECES[6])
+    send_home(0, 0)
+    hand_on(*PIECES[6])
     fwd1 = forward(1)
     take_in(*PIECES[7])
-    send_home(0, 0)
     send_home(0, 1)
-    back1 = backward(1, *fwd1)
-    relay(1, 1)
+    hand_on(*PIECES[7])
+    *back1, rows1 = backward(1, *fwd1)
+    reduce_rest(1, rows1)
+    send_home(1, 0)
     gate_home()
-    send_home(1, 0)
     send_home(1, 1)
     weight_grads(1, fwd1[0], *back1)
 

time: 106 us -> 105 us (level)
  no operation moved by 1% of the time
where the time goes in v4:
time: 105 us
  Pallas kernels  104 us (99%)
    pallas_call x1, Pallas kernels, body(): pl.pallas_call(functools.partial(kernel, n_src, n_half), out_shape=tuple(...  102 us
    pallas_call x1, Pallas kernels, body(): pl.pallas_call(write_out, out_shape=shapes, in_specs=[pl.BlockSpec(memory...  2.3 us

profile of v4, /device:TPU:1, one launch (start us, length us, event | category | flops | bytes accessed | tf_op | source)
XLA Modules:
  0.0 105.0 jit_solution(6262566565791061256)
XLA Ops:
  0.6 101.9 %experts_backward.1 = (bf16[256,512]{1,0:T(8,128)(2,1)S(1)}, bf16[2,192,2048]{2,1,0:T(8,128)(2,1)S(1)}, bf16[2,192,2048]{2,1,0:T(8,128)(2,1)S(1)}, bf16[2,192,2048]{2,1,0:T(8,128)(2,1)S(1)}, bf16[8,128]{1,0:T(8,128)(2,1)S(1)}) custom-call(bf16[256,512]{1,0:T(8,128)(2,1)} %tok_hbm.1, bf16[256,512]{1,0:T(8,128)(2,1)} %out_grad_hbm.1, s32[8,128]{1,0:T(8,128)} %bitcast.10, ...), custom_call_target="tpu_custom_call" | custom-call | flops 4000000000 | bytes 10000000 | tf_op jit(solution)/shard_map/experts_backward/pallas_call | solution.py:439
  102.5 2.3 %write_out.1 = (bf16[256,512]{1,0:T(8,128)(2,1)}, bf16[2,192,2048]{2,1,0:T(8,128)(2,1)}, bf16[2,192,2048]{2,1,0:T(8,128)(2,1)}, bf16[2,192,2048]{2,1,0:T(8,128)(2,1)}, bf16[8,128]{1,0:T(8,128)(2,1)}) custom-call(bf16[256,512]{1,0:T(8,128)(2,1)S(1)} %get-tuple-element.15.a, bf16[2,192,2048]{2,1,0:T(8,128)(2,1)S(1)} %get-tuple-element.16.b, ...), custom_call_target="tpu_custom_call" | custom-call | tf_op jit(solution)/shard_map/write_out/pallas_call | solution.py:481
